TPU v7x, 256 devices: a whole 4x4x8 slice. The times are simulated.
256 devices in a mesh: src: 8 (over x, core), tgt: 32 (over y, z).
Axes of the slice: x: 4, y: 4, z: 8, core: 2. Of those that a mesh axis runs over, the one named last changes fastest.
Arguments:
- source_embed: bfloat16 [16384, 256], P(('src', 'tgt'))
- source_links: int32 [16384, 8], P(('src', 'tgt')), may hold values from 0 to 2047
- source_degree: int32 [16384], P(('src', 'tgt')), may hold values from 1 to 8
- target_embed: bfloat16 [32768, 256], P('tgt')
- target_links: int32 [32768, 8], P('tgt'), may hold values from 0 to 1023
- target_degree: int32 [32768], P('tgt'), may hold values from 1 to 8
- w_self: bfloat16 [256, 256], replicated, may hold values from -0.375 to 0.375
- w_neigh: bfloat16 [256, 256], replicated, may hold values from -0.375 to 0.375
- cand_blocks: int32 [128, 32], P('src'), may hold values from 0 to 255, all different within a row; in each aligned block of 16 rows (0 to 15, 16 to 31, ...) at most 4 rows name the same one
- probe_pairs: int32 [16384, 16], P('src'), may hold values from 0 to 4095
Outputs:
- plan_scores: float32 [16384, 16], P(('src', 'tgt'))
Inputs may be any that keep to these rules, and one draw needn't show every extreme that they name: `source_links`: A neighbour index within the source entity's group of 2048 entities. `target_links`: A neighbour index within the target entity's block of 1024 entities. Only the first source_degree entries of a row count. Only the first target_degree entries of a row count. `cand_blocks`: the blocks of a row are distinct; within each aligned block of 16 rows (one group) no target block is named by more than 4 rows, and some target block is named by exactly 4; every target block is named by some row. `probe_pairs`: p names candidate block p // 128 of the row's source block and the target at offset p mod 128 in it.
All inputs are finite; a program needn't handle non-finite values.
Results may differ from a plain program's by a relative error of at most 0.0018.
Values may be sent and summed in bfloat16 or wider, within the bound.
A program may use at most 64 MiB of HBM per device.

v0:
```python
import math

import jax
import jax.numpy as jnp
from jax import lax
from jax.sharding import PartitionSpec as P

D = 256
BLK = 128
CAND = 32
MOST = 4
QRY = 16
SWEEPS = 4


NEG_FILL = -1e30


def aggregate(table, links, degree, own, w_self, w_neigh):
    table_rows = jnp.arange(table.shape[0], dtype=jnp.int32)
    adjacency = jnp.zeros((links.shape[0], table.shape[0]), jnp.bfloat16)
    for slot in range(links.shape[1]):
        hit = (links[:, slot][:, None] == table_rows[None, :]) & (slot < degree)[:, None]
        adjacency = adjacency + hit.astype(jnp.bfloat16)
    total = jnp.dot(adjacency, table, preferred_element_type=jnp.float32)
    mean_rows = (total / degree[:, None].astype(jnp.float32)).astype(jnp.bfloat16)
    mixed = jnp.dot(own, w_self, preferred_element_type=jnp.float32) + jnp.dot(
        mean_rows, w_neigh, preferred_element_type=jnp.float32
    )
    return mixed.astype(jnp.bfloat16)


def shards(
    source_embed,
    source_links,
    source_degree,
    target_embed,
    target_links,
    target_degree,
    w_self,
    w_neigh,
    cand_blocks,
    probe_pairs,
):
    group_count = lax.axis_size("src")
    member_index = lax.axis_index("tgt")
    group_x = lax.all_gather(source_embed, "tgt", axis=0, tiled=True)
    own_h = aggregate(group_x, source_links, source_degree, source_embed, w_self, w_neigh)
    group_h = lax.all_gather(own_h, "tgt", axis=0, tiled=True)
    target_rows = target_embed.shape[0]
    target_h = aggregate(target_embed, target_links, target_degree, target_embed, w_self, w_neigh)
    row_blocks = cand_blocks.shape[0]
    local_blocks = target_rows // BLK
    first_block = member_index * local_blocks
    block_ids = first_block + jnp.arange(local_blocks, dtype=jnp.int32)
    hits = jnp.any(cand_blocks[:, :, None] == block_ids[None, None, :], axis=1).astype(jnp.int32)
    before = jnp.cumsum(hits, axis=0) - hits
    slot_ids = jnp.arange(MOST, dtype=jnp.int32)
    chosen = hits[:, :, None] * (before[:, :, None] == slot_ids[None, None, :]).astype(jnp.int32)
    slot_valid = jnp.sum(chosen, axis=0)
    slot_row = jnp.sum(chosen * jnp.arange(row_blocks, dtype=jnp.int32)[:, None, None], axis=0)
    valid_mask = slot_valid > 0
    column_used = jnp.any(valid_mask, axis=1).astype(jnp.float32)
    slot_row_flat = slot_row.reshape(-1)
    select = chosen.reshape(row_blocks, local_blocks * MOST).astype(jnp.float32)
    select_mask = select > 0
    blocked_h = group_h.reshape(row_blocks, BLK * D)
    slot_rows_h = (
        jnp.dot(select.astype(jnp.bfloat16).T, blocked_h, preferred_element_type=jnp.float32)
        .astype(jnp.bfloat16)
        .reshape(local_blocks, MOST, BLK, D)
    )
    target_blocks = target_h.reshape(local_blocks, BLK, D)
    raw_scores = jnp.einsum(
        "cmad,cbd->cmab", slot_rows_h, target_blocks, preferred_element_type=jnp.float32
    ) * (3.0 / math.sqrt(D))
    filled = jnp.where(valid_mask[:, :, None, None], raw_scores, NEG_FILL)
    log_ratio = math.log(source_embed.shape[0] * group_count / target_rows)
    column_potential = jnp.zeros((local_blocks, BLK), jnp.float32)
    row_potential = jnp.zeros((row_blocks, BLK), jnp.float32)
    for sweep in range(SWEEPS):
        shifted = filled + column_potential[:, None, None, :]
        slot_max = jnp.max(shifted, axis=3)
        slot_sum = jnp.sum(jnp.exp(shifted - slot_max[..., None]), axis=3)
        flat_max = slot_max.reshape(-1, BLK)
        flat_sum = slot_sum.reshape(-1, BLK)
        block_max = jnp.max(
            jnp.where(select_mask[:, :, None], flat_max[None, :, :], NEG_FILL), axis=1
        )
        row_top = lax.pmax(block_max, "tgt")
        weights = flat_sum * jnp.exp(flat_max - jnp.take(row_top, slot_row_flat, axis=0))
        row_sum = lax.psum(jnp.dot(select, weights, precision=lax.Precision.HIGHEST), "tgt")
        row_potential = -(row_top + jnp.log(row_sum))
        slot_potential = jnp.take(row_potential, slot_row_flat, axis=0).reshape(
            local_blocks, MOST, BLK
        )
        shifted = filled + slot_potential[..., None]
        column_max = jnp.max(shifted, axis=(1, 2))
        column_sum = (
            jnp.sum(jnp.exp(shifted - column_max[:, None, None, :]), axis=(1, 2))
            * column_used[:, None]
        )
        column_top = lax.pmax(column_max, "src")
        column_total = lax.psum(column_sum * jnp.exp(column_max - column_top), "src")
        column_potential = log_ratio - (column_top + jnp.log(column_total))
    probe_rows = probe_pairs.reshape(row_blocks, BLK * QRY)
    which = probe_rows // BLK
    offset = probe_rows % BLK
    target_block = jnp.take_along_axis(cand_blocks, which, axis=1)
    local_index = target_block - first_block
    owned = (local_index >= 0) & (local_index < local_blocks)
    local_safe = jnp.clip(local_index, 0, local_blocks - 1)
    slot_of = jnp.clip(jnp.take_along_axis(before, local_safe, axis=1), 0, MOST - 1)
    inner = jnp.broadcast_to(
        (jnp.arange(BLK * QRY, dtype=jnp.int32) // QRY)[None, :], probe_rows.shape
    )
    flat_index = ((local_safe * MOST + slot_of) * BLK + inner) * BLK + offset
    picked = jnp.take(raw_scores.reshape(-1), flat_index)
    value = picked + jnp.take_along_axis(row_potential, inner, axis=1)
    value = (
        value
        + jnp.take(column_potential.reshape(-1), local_safe * BLK + offset)
        + math.log(CAND * BLK)
    )
    contrib = jnp.where(owned, value, 0.0).reshape(row_blocks * BLK, QRY)
    return lax.psum_scatter(contrib, "tgt", scatter_dimension=0, tiled=True)


def solution(mesh):
    placed = (
        P(("src", "tgt"), None),
        P(("src", "tgt"), None),
        P(("src", "tgt")),
        P("tgt", None),
        P("tgt", None),
        P("tgt"),
        P(),
        P(),
        P("src", None),
        P("src", None),
    )
    return jax.shard_map(
        shards, mesh=mesh, in_specs=placed, out_specs=P(("src", "tgt"), None), check_vma=False
    )
```

profile of v0, /device:TPU:1, one launch (start us, length us, event | category | flops | bytes accessed | tf_op | source)
XLA Modules:
  0.0 1951.3 jit_solution(720900429715428418)
XLA Ops:
  11.1 209.9 %gather_fusion.2 = s32[32768]{0:T(1024)S(1)} fusion(s32[16,32]{1,0:T(8,128)S(1)} %copy-done.1, s32[32768]{0:T(1024)S(1)} %bitcast.91), kind=kCustom, calls=%fused_computation.10 | custom fusion | bytes 524288 | tf_op jit(solution)/shard_map/jit(take_along_axis)/gather | solution.py:109
  221.2 209.9 %gather_fusion.3 = s32[32768]{0:T(1024)S(1)} fusion(s32[16,8]{1,0:T(8,128)S(1)} %convert_subtract_fusion, s32[32768]{0:T(1024)S(1)} %bitcast.90), kind=kCustom, calls=%fused_computation.11 | custom fusion | bytes 524288 | tf_op jit(solution)/shard_map/jit(take_along_axis)/gather | solution.py:113
  435.2 1.4 broadcast_in_dim.191
  439.1 2.9 fusion.50
  442.3 7.7 fusion.48
  450.0 67.8 %all-gather.5.cloned.1.call-done = bf16[2048,256]{1,0:T(8,128)(2,1)} async-done(((bf16[64,256]{1,0:T(8,128)(2,1)}), bf16[2048,256]{1,0:T(8,128)(2,1)}) %all-gather.5.cloned.1.call-update) | async-done | bytes 1048592 | tf_op jit(solution)/shard_map/all_gather | solution.py:49
  517.7 1.6 reshape.571
  522.0 59.0 %pmax.56 = f32[16,128]{1,0:T(8,128)S(1)} all-reduce(f32[16,128]{1,0:T(8,128)S(1)} %select_reduce_fusion.3), channel_id=1, replica_groups=mesh['src'=8,'tgt'=32] {'tgt'}, use_global_device_ids=true, to_apply=%region_5.6 | all-reduce | flops 2048 | bytes 16384 | tf_op jit(solution)/shard_map/pmax | solution.py:90
  583.2 57.1 %psum.56 = f32[16,128]{1,0:T(8,128)S(1)} all-reduce(f32[16,128]{1,0:T(8,128)S(1)} %fusion.150), channel_id=1, replica_groups=mesh['src'=8,'tgt'=32] {'tgt'}, use_global_device_ids=true, to_apply=%region_8.10 | all-reduce | flops 2048 | bytes 16384 | tf_op jit(solution)/shard_map/psum | solution.py:92
  642.5 44.7 %pmax.57 = f32[8,128]{1,0:T(8,128)S(1)} all-reduce(f32[8,128]{1,0:T(8,128)S(1)} %add_reduce_fusion.6), channel_id=1, replica_groups=mesh['src'=8,'tgt'=32] {'src'}, use_global_device_ids=true, to_apply=%region_10.12 | all-reduce | flops 1024 | bytes 8192 | tf_op jit(solution)/shard_map/pmax | solution.py:103
  687.3 12.6 psum.57
  700.7 1.4 exponential_reduce_fusion.5
  702.3 58.4 %pmax.58 = f32[16,128]{1,0:T(8,128)S(1)} all-reduce(f32[16,128]{1,0:T(8,128)S(1)} %select_reduce_fusion.2), channel_id=1, replica_groups=mesh['src'=8,'tgt'=32] {'tgt'}, use_global_device_ids=true, to_apply=%region_16.18 | all-reduce | flops 2048 | bytes 16384 | tf_op jit(solution)/shard_map/pmax | solution.py:90
  761.5 57.1 %psum.58 = f32[16,128]{1,0:T(8,128)S(1)} all-reduce(f32[16,128]{1,0:T(8,128)S(1)} %fusion.146), channel_id=1, replica_groups=mesh['src'=8,'tgt'=32] {'tgt'}, use_global_device_ids=true, to_apply=%region_18.20 | all-reduce | flops 2048 | bytes 16384 | tf_op jit(solution)/shard_map/psum | solution.py:92
  820.8 40.2 %pmax.59 = f32[8,128]{1,0:T(8,128)S(1)} all-reduce(f32[8,128]{1,0:T(8,128)S(1)} %add_reduce_fusion.4), channel_id=1, replica_groups=mesh['src'=8,'tgt'=32] {'src'}, use_global_device_ids=true, to_apply=%region_20.22 | all-reduce | flops 1024 | bytes 8192 | tf_op jit(solution)/shard_map/pmax | solution.py:103
  861.1 12.4 psum.59
  874.2 1.4 exponential_reduce_fusion.3
  875.8 58.4 %pmax.60 = f32[16,128]{1,0:T(8,128)S(1)} all-reduce(f32[16,128]{1,0:T(8,128)S(1)} %select_reduce_fusion.1), channel_id=1, replica_groups=mesh['src'=8,'tgt'=32] {'tgt'}, use_global_device_ids=true, to_apply=%region_25.27 | all-reduce | flops 2048 | bytes 16384 | tf_op jit(solution)/shard_map/pmax | solution.py:90
  935.0 56.8 %psum.60 = f32[16,128]{1,0:T(8,128)S(1)} all-reduce(f32[16,128]{1,0:T(8,128)S(1)} %fusion.142), channel_id=1, replica_groups=mesh['src'=8,'tgt'=32] {'tgt'}, use_global_device_ids=true, to_apply=%region_27.29 | all-reduce | flops 2048 | bytes 16384 | tf_op jit(solution)/shard_map/psum | solution.py:92
  994.0 40.5 %pmax.61 = f32[8,128]{1,0:T(8,128)S(1)} all-reduce(f32[8,128]{1,0:T(8,128)S(1)} %add_reduce_fusion.2), channel_id=1, replica_groups=mesh['src'=8,'tgt'=32] {'src'}, use_global_device_ids=true, to_apply=%region_29.31 | all-reduce | flops 1024 | bytes 8192 | tf_op jit(solution)/shard_map/pmax | solution.py:103
  1034.6 12.4 psum.61
  1047.7 1.4 exponential_reduce_fusion.1
  1049.3 58.4 %pmax.62 = f32[16,128]{1,0:T(8,128)S(1)} all-reduce(f32[16,128]{1,0:T(8,128)S(1)} %select_reduce_fusion), channel_id=1, replica_groups=mesh['src'=8,'tgt'=32] {'tgt'}, use_global_device_ids=true, to_apply=%region_34.36 | all-reduce | flops 2048 | bytes 16384 | tf_op jit(solution)/shard_map/pmax | solution.py:90
  1108.5 56.8 %psum.62 = f32[16,128]{1,0:T(8,128)S(1)} all-reduce(f32[16,128]{1,0:T(8,128)S(1)} %fusion.138), channel_id=1, replica_groups=mesh['src'=8,'tgt'=32] {'tgt'}, use_global_device_ids=true, to_apply=%region_36.38 | all-reduce | flops 2048 | bytes 16384 | tf_op jit(solution)/shard_map/psum | solution.py:92
  1167.5 40.5 %pmax.63 = f32[8,128]{1,0:T(8,128)S(1)} all-reduce(f32[8,128]{1,0:T(8,128)S(1)} %add_reduce_fusion), channel_id=1, replica_groups=mesh['src'=8,'tgt'=32] {'src'}, use_global_device_ids=true, to_apply=%region_38.40 | all-reduce | flops 1024 | bytes 8192 | tf_op jit(solution)/shard_map/pmax | solution.py:103
  1208.0 180.5 %gather_fusion = f32[32768]{0:T(1024)S(1)} fusion(f32[524288]{0:T(1024)S(1)} %bitcast.88, s32[32768]{0:T(1024)S(1)} %broadcast_clamp_fusion.1), kind=kCustom, calls=%fused_computation.8 | custom fusion | bytes 393216 | tf_op jit(solution)/shard_map/jit(_take)/gather | solution.py:118
  1389.9 201.1 %gather_fusion.4 = f32[32768]{0:T(1024)S(1)} fusion(f32[16,128]{1,0:T(8,128)S(1)} %add_negate_fusion, s32[32768]{0:T(1024)S(1)} %bitcast.89), kind=kCustom, calls=%fused_computation.12 | custom fusion | bytes 524288 | tf_op jit(solution)/shard_map/jit(take_along_axis)/gather | solution.py:119
  1592.4 12.4 psum.63
  1604.9 130.0 %gather_fusion.1 = f32[32768]{0:T(1024)S(1)} fusion(f32[1024]{0:T(1024)S(1)} %subtract_bitcast_fusion, s32[32768]{0:T(1024)S(1)} %broadcast_clamp_fusion), kind=kCustom, calls=%fused_computation.9 | custom fusion | bytes 393216 | tf_op jit(solution)/shard_map/jit(_take)/gather | solution.py:122
  1736.2 5.6 add_select_fusion.2
  1741.8 201.6 %reduce-scatter.2.cloned.1.call-done = f32[64,16]{1,0:T(8,128)} async-done(((f32[2048,16]{1,0:T(8,128)}), f32[64,16]{1,0:T(8,128)}) %reduce-scatter.2.cloned.1.call-update) | async-done | bytes 4112 | tf_op jit(solution)/shard_map/reduce_scatter | solution.py:126
  1943.3 1.4 copy.28
  (134 shorter events, 34.1 us)
Async XLA Ops:
  6.5 432.1 %copy-start = (bf16[1024,256]{1,0:T(8,128)(2,1)S(1)}, bf16[1024,256]{1,0:T(8,128)(2,1)}, u32[]{:S(2)}) copy-start(bf16[1024,256]{1,0:T(8,128)(2,1)} %param.15) | copy-start | bytes 1572868
  6.5 4.5 copy-start.1
  6.5 432.5 %all-gather.3.cloned.1.call-start = ((), (), s32[]{:S(2)}) async-start(), calls=%async_computation.1 | async-start | bytes 1081344 | tf_op jit(solution)/shard_map/all_gather | solution.py:47
  7.3 510.5 %all-gather.5.cloned.1.call-start = ((), (), s32[]{:S(2)}) async-start(), calls=%async_computation.2 | async-start | bytes 1081344 | tf_op jit(solution)/shard_map/all_gather | solution.py:49
  9.9 1.0 copy-start.2
  431.1 2.7 copy-start.9
  431.2 2.7 copy-start.10
  431.2 2.7 copy-start.8
  434.6 3.8 copy-start.7
  434.7 3.8 copy-start.5
  434.7 3.8 copy-start.6
  436.6 2.4 copy-start.11
  442.0 1501.3 %reduce-scatter.2.cloned.1.call-start = ((), (), s32[]{:S(2)}) async-start(), calls=%async_computation.3 | async-start | bytes 1081344 | tf_op jit(solution)/shard_map/reduce_scatter | solution.py:126
  520.0 1.0 copy-start.12
  1604.8 131.4 %copy-start.3 = (s32[2048,16]{1,0:T(8,128)S(1)}, s32[2048,16]{1,0:T(8,128)}, u32[]{:S(2)}) copy-start(s32[2048,16]{1,0:T(8,128)} %copy-done.2) | copy-start | bytes 393220
  1604.8 131.4 %copy-start.4 = (s32[2048,16]{1,0:T(8,128)S(1)}, s32[2048,16]{1,0:T(8,128)}, u32[]{:S(2)}) copy-start(s32[2048,16]{1,0:T(8,128)} %gather.41) | copy-start | bytes 393220
Sparse Core Ops, SparseCore 0:
  10.0 75.5 all-gather.2
  442.1 75.5 all-gather.4
  1741.9 201.3 reduce-scatter.1
where the time goes:
time: 1960 us; the launch traced here: 1950 us
  local copies, waits for them, and re-layouts  953 us (49%)
  blocking collectives  678 us (35%)
  waiting for transfers between devices  270 us (14%)
  other arithmetic  23 us (1%)
    pmax x4, blocking collectives, shards(): row_top = lax.pmax(block_max, 'tgt')  234 us
    psum x4, blocking collectives, shards(): lax.psum(jnp.dot(select, weights, precision=lax.Precision.HIGHEST), 'tgt')  228 us
    gather x3, local copies, waits for them, and re-layouts, shards(): target_block = jnp.take_along_axis(cand_blocks, which, axis=1)  211 us
    gather x3, local copies, waits for them, and re-layouts, shards(): jnp.take_along_axis(before, local_safe, axis=1)  211 us
    gather x2, local copies, waits for them, and re-layouts, shards(): value = picked + jnp.take_along_axis(row_potential, inner, axis=1)  202 us
    reduce_scatter x1, waiting for transfers between devices, shards(): return lax.psum_scatter(contrib, 'tgt', scatter_dimension=0, tiled=True)  202 us
    gather x2, local copies, waits for them, and re-layouts, shards(): picked = jnp.take(raw_scores.reshape(-1), flat_index)  182 us
    pmax x4, blocking collectives, shards(): column_top = lax.pmax(column_max, 'src')  166 us
  transfers between devices with their start and end apart: 3, of which 2 were waited for; matrix products, arithmetic and copies ran while one was open for 22% of the time, Pallas kernels for 0%

commit v1 on v0

v1 whole, which is shorter than its diff:
```python
import functools
import math

import jax
import jax.numpy as jnp
from jax import lax
from jax.experimental import pallas as pl
from jax.experimental.pallas import tpu as pltpu
from jax.sharding import PartitionSpec as P

D = 256
BLK = 128
CAND = 32
MOST = 4
QRY = 16
SWEEPS = 4
KMAX = 8
NY, NZ = 4, 8
NSRC, NTGT = 8, 32
ROWS = 64
R_BLK = 16
C_LOC = 8
SLOTS = C_LOC * MOST
A_ROWS = 48
B_ROWS = 16
WIDE = 256
NEG = -1e30
FLOOR = -1e29
SCALE = 3.0 / math.sqrt(D)
MESH = pl.DeviceIdType.MESH
BF = jnp.bfloat16
F32 = jnp.float32


def far_first():
    offs = [(dy, dz) for dy in range(NY) for dz in range(NZ) if (dy, dz) != (0, 0)]
    dist = lambda o: min(o[0], NY - o[0]) + min(o[1], NZ - o[1])
    return sorted(offs, key=lambda o: (-dist(o), o))


Z_FAR = (4, 3, 5, 2, 6, 1, 7)
Z_NEAR = (1, 7, 2, 6, 3, 5, 4)
Y_FAR = (2, 1, 3)


def sinkhorn_kernel(
    srow_ref, place_ref, x_ref, sl_ref, t_ref, tl_ref, ws_ref, wn_ref, tab_ref, pp_ref,
    out_ref,
    iota_ref, big_x, xt_ref, lk_ref, at_ref, ht_ref, tt_ref, att_ref, th_ref,
    s_ref, e_ref, wb_ref, rx_ref, cx_ref, top_ref, r0_ref, u_ref, sid_ref, g_ref, pk_ref,
    fs_ref, fr_ref,
    a_send, a_recv, b_send, b_recv, ya_send, ya_recv, zb_send, zb_recv, lk_send, lk_recv,
    r_send, r_recv, c_send, c_recv, f_send, f_recv,
):
    s = lax.axis_index("src")
    t = lax.axis_index("tgt")
    y = t // NZ
    z = lax.rem(t, NZ)
    tgt_peers = [lax.rem(y + dy, NY) * NZ + lax.rem(z + dz, NZ) for dy, dz in far_first()]
    sx = s // 2
    score = lax.rem(s, 2)
    src_peers = [
        lax.rem(sx + dx, 4) * 2 + (score if same else 1 - score)
        for dx, same in ((2, False), (2, True), (1, False), (3, False), (1, True), (3, True), (0, False))
    ]

    barrier = pltpu.get_barrier_semaphore()
    for p in tgt_peers:
        pl.semaphore_signal(barrier, inc=1, device_id=(s, p), device_id_type=MESH)
    for p in src_peers:
        pl.semaphore_signal(barrier, inc=1, device_id=(p, t), device_id_type=MESH)

    tile_rows = lax.broadcasted_iota(jnp.int32, (WIDE // 16, 16, BLK), 0) * 16
    tile_rows = tile_rows + lax.broadcasted_iota(jnp.int32, (WIDE // 16, 16, BLK), 1)
    iota_ref[...] = tile_rows.astype(F32).astype(BF)
    lane8 = lax.broadcasted_iota(jnp.int32, (KMAX, BLK), 1)
    big_x[pl.ds(t * ROWS, ROWS), :] = x_ref[...]
    lk_ref[t] = jnp.where((lane8 // ROWS) == lax.rem(t, 2), sl_ref[...], 0)
    g_ref[SLOTS] = jnp.zeros((QRY, BLK), F32)

    pl.semaphore_wait(barrier, NTGT - 1 + NSRC - 1)

    def push(src, dst, ssem, rsem, dev):
        pltpu.make_async_remote_copy(
            src_ref=src, dst_ref=dst, send_sem=ssem, recv_sem=rsem, device_id=dev, device_id_type=MESH
        ).start()

    def drain(ref, sem):
        pltpu.make_async_copy(ref, ref, sem).wait()

    def part_a(d):
        return big_x.at[pl.ds(d * ROWS, A_ROWS)]

    def part_b(d):
        return big_x.at[pl.ds(d * ROWS + A_ROWS, B_ROWS)]

    def at_yz(dy, dz):
        return lax.rem(y + dy + NY, NY) * NZ + lax.rem(z + dz + NZ, NZ)

    for k in Z_FAR:
        push(part_a(t), part_a(t), a_send, a_recv.at[k], (s, at_yz(0, k)))
    for j in Y_FAR:
        push(part_b(t), part_b(t), b_send, b_recv.at[j], (s, at_yz(j, 0)))
    for p in tgt_peers:
        push(lk_ref.at[t], lk_ref.at[t], lk_send, lk_recv, (s, p))
    for j in Y_FAR:
        push(part_a(t), part_a(t), ya_send, ya_recv, (s, at_yz(j, 0)))
    for k in Z_FAR:
        push(part_b(t), part_b(t), zb_send, zb_recv, (s, at_yz(0, k)))

    ws_t = ws_ref[...].T
    wn_t = wn_ref[...].T
    for chunk in range(4):
        tt_ref[:, chunk * WIDE : (chunk + 1) * WIDE] = t_ref[chunk * WIDE : (chunk + 1) * WIDE, :].T

    for j in Y_FAR[::-1]:
        drain(part_b(t), b_recv.at[j])
        d = at_yz(-j, 0)
        for k in Z_FAR:
            push(part_b(d), part_b(d), zb_send, zb_recv, (s, at_yz(0, k)))
    for k in Z_NEAR:
        drain(part_a(t), a_recv.at[k])
        d = at_yz(0, -k)
        for j in Y_FAR:
            push(part_a(d), part_a(d), ya_send, ya_recv, (s, at_yz(j, 0)))

    def build(links, chunks, put):
        def body(q, _):
            base = (q * WIDE).astype(F32)
            near = jnp.clip(links - base, -1.0, float(WIDE))
            total = jnp.zeros((WIDE // 16, 16, BLK), BF)
            for k in range(KMAX):
                row = jnp.broadcast_to(near[k : k + 1, :], (16, BLK)).astype(BF)
                total = total + jnp.where(row[None] == iota_ref[...], 1.0, 0.0).astype(BF)
            put(q, total.reshape(WIDE, BLK))
            return 0

        lax.fori_loop(0, chunks, body, 0)

    def encode(table_t, adjacency, own_t, degree):
        total = jnp.dot(table_t, adjacency, preferred_element_type=F32)
        mean = (total / degree).astype(BF)
        mixed = jnp.dot(ws_t, own_t, preferred_element_type=F32) + jnp.dot(
            wn_t, mean, preferred_element_type=F32
        )
        return mixed.astype(BF)

    for chunk in range(4):
        cols = slice(chunk * WIDE, (chunk + 1) * WIDE)
        links = tl_ref[:, cols]
        degree = jnp.sum((links >= 0).astype(F32), axis=0, keepdims=True)
        for half in range(2):
            def put(q, value, half=half):
                att_ref[pl.ds(q * WIDE, WIDE), half * BLK : (half + 1) * BLK] = value

            build(links[:, half * BLK : (half + 1) * BLK].astype(F32), 4, put)
        coded = encode(tt_ref[...], att_ref[...], tt_ref[:, cols], degree).T
        th_ref[2 * chunk] = coded[:BLK]
        th_ref[2 * chunk + 1] = coded[BLK:]

    drain(lk_ref.at[pl.ds(0, NTGT - 1)], lk_recv)

    def group_links(block):
        return lk_ref[2 * block] + lk_ref[2 * block + 1]

    def build_pair(pair, _):
        for half in range(2):
            def put(q, value, half=half):
                at_ref[pair, pl.ds(q * WIDE, WIDE), half * BLK : (half + 1) * BLK] = value

            build(group_links(2 * pair + half).astype(F32), 8, put)
        return 0

    lax.fori_loop(0, 8, build_pair, 0)

    drain(big_x.at[pl.ds(0, 24 * A_ROWS)], ya_recv)
    drain(big_x.at[pl.ds(0, 28 * B_ROWS)], zb_recv)
    for chunk in range(8):
        xt_ref[chunk] = big_x[chunk * WIDE : (chunk + 1) * WIDE, :].T

    def encode_pair(pair, _):
        links = jnp.concatenate([group_links(2 * pair), group_links(2 * pair + 1)], axis=1)
        degree = jnp.sum((links >= 0).astype(F32), axis=0, keepdims=True)
        total = jnp.zeros((D, WIDE), F32)
        for q in range(8):
            total = total + jnp.dot(
                xt_ref[q], at_ref[pair, q * WIDE : (q + 1) * WIDE, :], preferred_element_type=F32
            )
        mean = (total / degree).astype(BF)
        mixed = jnp.dot(ws_t, xt_ref[pair], preferred_element_type=F32) + jnp.dot(
            wn_t, mean, preferred_element_type=F32
        )
        coded = mixed.astype(BF)
        ht_ref[2 * pair] = coded[:, :BLK]
        ht_ref[2 * pair + 1] = coded[:, BLK:]
        return 0

    lax.fori_loop(0, 8, encode_pair, 0)

    block_id = lax.broadcasted_iota(jnp.int32, (R_BLK, BLK), 0)
    lane = lax.broadcasted_iota(jnp.int32, (BLK, BLK), 1)
    neg16 = jnp.full((R_BLK, BLK), NEG, F32)

    def score_block(c, best):
        for m in range(MOST):
            r = srow_ref[c * MOST + m]
            bias = jnp.where(r < 0, NEG, 0.0)
            raw = jnp.dot(th_ref[c], ht_ref[jnp.maximum(r, 0)], preferred_element_type=F32)
            raw = raw * SCALE + bias
            s_ref[c * MOST + m] = raw
            best = jnp.maximum(best, jnp.where(block_id == r, jnp.max(raw, axis=0, keepdims=True), NEG))
        return best

    top = lax.fori_loop(0, C_LOC, score_block, neg16)
    top_ref[...] = top

    def first_rows(c, total):
        for m in range(MOST):
            r = srow_ref[c * MOST + m]
            high = top_ref[pl.ds(jnp.maximum(r, 0), 1), :]
            part = jnp.sum(jnp.exp(s_ref[c * MOST + m] - high), axis=0, keepdims=True)
            total = total + jnp.where(block_id == r, part, 0.0)
        return total

    total = lax.fori_loop(0, C_LOC, first_rows, jnp.zeros((R_BLK, BLK), F32))
    rx_ref[0, t] = jnp.where(total > 0.0, top + jnp.log(total), NEG)

    def send_rows(sweep):
        for p in tgt_peers:
            push(rx_ref.at[sweep, t], rx_ref.at[sweep, t], r_send.at[sweep], r_recv.at[sweep], (s, p))

    def await_rows(sweep):
        drain(rx_ref.at[sweep, pl.ds(0, NTGT - 1)], r_recv.at[sweep])
        return rx_ref[sweep]

    def send_cols(sweep):
        for p in src_peers:
            push(cx_ref.at[sweep, s], cx_ref.at[sweep, s], c_send.at[sweep], c_recv.at[sweep], (p, t))

    def await_cols(sweep):
        drain(cx_ref.at[sweep, pl.ds(0, NSRC - 1)], c_recv.at[sweep])
        return cx_ref[sweep]

    send_rows(0)

    def probe_slots(block, _):
        table = jnp.broadcast_to(tab_ref[block], (8, BLK))
        for half in range(2):
            rows = slice(half * 8, half * 8 + 8)
            which = pp_ref[block, rows, :] // BLK
            sid_ref[block, rows, :] = jnp.take_along_axis(table, which, axis=1)
        return 0

    lax.fori_loop(0, R_BLK, probe_slots, 0)

    def pick(slot, _):
        r = jnp.maximum(srow_ref[slot], 0)
        for half in range(2):
            rows = slice(half * 8, half * 8 + 8)
            offset = lax.rem(pp_ref[r, rows, :], BLK)
            strip, inner = offset // 8, lax.rem(offset, 8)
            value = jnp.zeros((8, BLK), F32)
            for k in range(BLK // 8):
                got = jnp.take_along_axis(s_ref[slot, k * 8 : k * 8 + 8, :], inner, axis=0)
                value = jnp.where(strip == k, got, value)
            g_ref[slot, rows, :] = jnp.where(sid_ref[r, rows, :] == slot, value, 0.0)
        return 0

    lax.fori_loop(0, SLOTS, pick, 0)

    def merge(block, _):
        total = jnp.zeros((QRY, BLK), F32)
        for c in range(C_LOC):
            total = total + g_ref[place_ref[block * C_LOC + c]]
        pk_ref[block] = total
        return 0

    lax.fori_loop(0, R_BLK, merge, 0)

    parts = await_rows(0)
    high = jnp.max(parts, axis=0)
    r0 = -(high + jnp.log(jnp.sum(jnp.exp(parts - high[None]), axis=0)))
    r0_ref[...] = r0

    def first_cols(c, carry):
        tops, sums = carry
        shifted = [
            s_ref[c * MOST + m] + r0_ref[pl.ds(jnp.maximum(srow_ref[c * MOST + m], 0), 1), :]
            for m in range(MOST)
        ]
        high = functools.reduce(jnp.maximum, shifted)
        high = jnp.maximum(jnp.max(high, axis=1, keepdims=True), FLOOR)
        total = jnp.zeros((BLK, BLK), F32)
        for m in range(MOST):
            e = jnp.exp(shifted[m] - high)
            e_ref[c * MOST + m] = e
            total = total + e
        total = jnp.sum(total, axis=1, keepdims=True)
        return jnp.where(lane == c, high, tops), jnp.where(lane == c, total, sums)

    zero_tile = jnp.zeros((BLK, BLK), F32)
    tops, sums = lax.fori_loop(0, C_LOC, first_cols, (zero_tile, zero_tile))
    tops = tops.T[:C_LOC]
    sums = sums.T[:C_LOC]
    cx_ref[0, s] = jnp.where(sums > 0.0, tops + jnp.log(sums), NEG)
    send_cols(0)
    parts = await_cols(0)
    high = jnp.max(parts, axis=0)
    share = R_BLK * BLK * NSRC / (C_LOC * BLK * NTGT)
    c0 = math.log(share) - (high + jnp.log(jnp.sum(jnp.exp(parts - high[None]), axis=0)))
    factor = jnp.exp(tops + c0)

    def spread(weights):
        upright = jnp.concatenate([weights, jnp.zeros((BLK - C_LOC, BLK), F32)], axis=0).T
        for c in range(C_LOC):
            wb_ref[c] = jnp.broadcast_to(upright[:, c : c + 1], (BLK, BLK))

    def sweep_body(sweep, carry):
        _, col_scale = carry
        spread(factor * col_scale)

        def rows_of(c, total):
            for m in range(MOST):
                part = jnp.sum(e_ref[c * MOST + m] * wb_ref[c], axis=0, keepdims=True)
                total = total + jnp.where(block_id == srow_ref[c * MOST + m], part, 0.0)
            return total

        rx_ref[sweep, t] = lax.fori_loop(0, C_LOC, rows_of, jnp.zeros((R_BLK, BLK), F32))
        send_rows(sweep)
        row_scale = 1.0 / jnp.sum(await_rows(sweep), axis=0)
        u_ref[...] = row_scale

        def cols_of(c, sums):
            total = jnp.zeros((BLK, BLK), F32)
            for m in range(MOST):
                r = jnp.maximum(srow_ref[c * MOST + m], 0)
                total = total + e_ref[c * MOST + m] * u_ref[pl.ds(r, 1), :]
            return jnp.where(lane == c, jnp.sum(total, axis=1, keepdims=True), sums)

        sums = lax.fori_loop(0, C_LOC, cols_of, zero_tile).T[:C_LOC]
        cx_ref[sweep, s] = sums * factor
        send_cols(sweep)
        return row_scale, share / jnp.sum(await_cols(sweep), axis=0)

    row_scale, col_scale = lax.fori_loop(
        1, SWEEPS, sweep_body, (jnp.ones((R_BLK, BLK), F32), jnp.ones((C_LOC, BLK), F32))
    )
    row_pot = r0 + jnp.log(row_scale)
    col_pot = c0 + jnp.log(col_scale) + math.log(CAND * BLK)
    u_ref[...] = row_pot
    top_ref[:C_LOC, :] = col_pot
    lane8 = lax.broadcasted_iota(jnp.int32, (8, BLK), 1)

    def finish(block, _):
        done = []
        for half in range(2):
            rows = slice(half * 8, half * 8 + 8)
            sid = sid_ref[block, rows, :]
            offset = lax.rem(pp_ref[block, rows, :], BLK)
            owner = sid // MOST
            value = jnp.zeros((8, BLK), F32)
            for c in range(C_LOC):
                strip = jnp.broadcast_to(top_ref[c : c + 1, :], (8, BLK))
                value = jnp.where(owner == c, jnp.take_along_axis(strip, offset, axis=1), value)
            value = value + pk_ref[block, rows, :] + u_ref[pl.ds(block, 1), :]
            done.append(jnp.where(sid >= 0, value, 0.0))
        low, high = done
        fs_ref[2 * block] = jnp.where(lane8 < ROWS, low, pltpu.roll(high, ROWS, 1))
        fs_ref[2 * block + 1] = jnp.where(lane8 < ROWS, pltpu.roll(low, ROWS, 1), high)
        return 0

    lax.fori_loop(0, R_BLK, finish, 0)
    for p in tgt_peers:
        push(fs_ref.at[p], fr_ref.at[t], f_send, f_recv, (s, p))
    fr_ref[t] = fs_ref[t]
    drain(fr_ref.at[pl.ds(0, NTGT - 1)], f_recv)
    out_ref[...] = jnp.sum(fr_ref[...], axis=0)

    drain(big_x.at[pl.ds(0, 7 * A_ROWS)], a_send)
    drain(big_x.at[pl.ds(0, 3 * B_ROWS)], b_send)
    drain(big_x.at[pl.ds(0, 24 * A_ROWS)], ya_send)
    drain(big_x.at[pl.ds(0, 28 * B_ROWS)], zb_send)
    drain(lk_ref.at[pl.ds(0, NTGT - 1)], lk_send)
    for sweep in range(SWEEPS):
        drain(rx_ref.at[sweep, pl.ds(0, NTGT - 1)], r_send.at[sweep])
        drain(cx_ref.at[sweep, pl.ds(0, NSRC - 1)], c_send.at[sweep])
    drain(fs_ref.at[pl.ds(0, NTGT - 1)], f_send)


def shards(
    source_embed,
    source_links,
    source_degree,
    target_embed,
    target_links,
    target_degree,
    w_self,
    w_neigh,
    cand_blocks,
    probe_pairs,
):
    slots = jnp.arange(KMAX, dtype=jnp.int32)[None, :]
    sl = jnp.where(slots < source_degree[:, None], source_links, -1).T
    sl = jnp.concatenate([sl, sl], axis=1)
    tl = jnp.where(slots < target_degree[:, None], target_links, -1).T
    pp = probe_pairs.reshape(R_BLK, BLK, QRY).transpose(0, 2, 1)

    local = cand_blocks - lax.axis_index("tgt") * C_LOC
    ids = jnp.arange(C_LOC, dtype=jnp.int32)
    match = local[:, :, None] == ids[None, None, :]
    hits = jnp.any(match, axis=1)
    blocks = jnp.arange(R_BLK, dtype=jnp.int32)
    earlier = blocks[None, :] < blocks[:, None]
    before = jnp.sum((earlier[:, :, None] & hits[None, :, :]).astype(jnp.int32), axis=1)
    place = jnp.where(hits, ids[None, :] * MOST + before, SLOTS)
    slot_ids = jnp.arange(SLOTS, dtype=jnp.int32)
    srow = jnp.sum(
        jnp.where(place.reshape(R_BLK, C_LOC, 1) == slot_ids[None, None, :], blocks[:, None, None] + 1, 0),
        axis=(0, 1),
    ) - 1
    tab = jnp.sum(jnp.where(match, place[:, None, :] + 1, 0), axis=2) - 1
    tab = jnp.pad(tab, ((0, 0), (0, BLK - CAND)), constant_values=-1).reshape(R_BLK, 1, BLK)

    vmem = pl.BlockSpec(memory_space=pltpu.VMEM)
    smem = pl.BlockSpec(memory_space=pltpu.SMEM)
    dma = pltpu.SemaphoreType.DMA
    packed = pl.pallas_call(
        sinkhorn_kernel,
        out_shape=jax.ShapeDtypeStruct((8, BLK), F32),
        in_specs=[smem, smem] + [vmem] * 8,
        out_specs=vmem,
        scratch_shapes=[
            pltpu.VMEM((WIDE // 16, 16, BLK), BF),
            pltpu.VMEM((NTGT * ROWS, D), BF),
            pltpu.VMEM((8, D, WIDE), BF),
            pltpu.VMEM((NTGT, KMAX, BLK), jnp.int32),
            pltpu.VMEM((8, NTGT * ROWS, WIDE), BF),
            pltpu.VMEM((R_BLK, D, BLK), BF),
            pltpu.VMEM((D, C_LOC * BLK), BF),
            pltpu.VMEM((C_LOC * BLK, WIDE), BF),
            pltpu.VMEM((C_LOC, BLK, D), BF),
            pltpu.VMEM((SLOTS, BLK, BLK), F32),
            pltpu.VMEM((SLOTS, BLK, BLK), F32),
            pltpu.VMEM((C_LOC, BLK, BLK), F32),
            pltpu.VMEM((SWEEPS, NTGT, R_BLK, BLK), F32),
            pltpu.VMEM((SWEEPS, NSRC, C_LOC, BLK), F32),
            pltpu.VMEM((R_BLK, BLK), F32),
            pltpu.VMEM((R_BLK, BLK), F32),
            pltpu.VMEM((R_BLK, BLK), F32),
            pltpu.VMEM((R_BLK, QRY, BLK), jnp.int32),
            pltpu.VMEM((SLOTS + 1, QRY, BLK), F32),
            pltpu.VMEM((R_BLK, QRY, BLK), F32),
            pltpu.VMEM((NTGT, 8, BLK), F32),
            pltpu.VMEM((NTGT, 8, BLK), F32),
            dma, dma((NZ,)), dma, dma((NY,)), dma, dma, dma, dma, dma, dma,
            dma((SWEEPS,)), dma((SWEEPS,)), dma((SWEEPS,)), dma((SWEEPS,)), dma, dma,
        ],
        compiler_params=pltpu.CompilerParams(
            collective_id=0, has_side_effects=True, vmem_limit_bytes=48 * 2**20
        ),
    )(
        srow, place.reshape(-1), source_embed, sl, target_embed, tl, w_self, w_neigh, tab, pp
    )
    return packed.reshape(8, 2, ROWS).transpose(2, 1, 0).reshape(ROWS, QRY)


def solution(mesh):
    placed = (
        P(("src", "tgt"), None),
        P(("src", "tgt"), None),
        P(("src", "tgt")),
        P("tgt", None),
        P("tgt", None),
        P("tgt"),
        P(),
        P(),
        P("src", None),
        P("src", None),
    )
    return jax.shard_map(
        shards, mesh=mesh, in_specs=placed, out_specs=P(("src", "tgt"), None), check_vma=False
    )
```

time: 1960 us -> 145 us (0.07)
  local copies, waits for them, and re-layouts: 953 us -> 4.75 us
  blocking collectives: 678 us -> 0 us
  waiting for transfers between devices: 270 us -> 0 us
  Pallas kernels: 0 us -> 139 us
  other arithmetic: 23 us -> 1.04 us
    gather x20 -> x0, local copies, waits for them, and re-layouts: 943 us -> none  [the longest x3 211 us: shards(): target_block = jnp.take_along_axis(cand_blocks, which, axis=1)]
    pmax x8 -> x0, blocking collectives: 400 us -> none  [the longest x4 234 us: shards(): row_top = lax.pmax(block_max, 'tgt')]
    psum x8 -> x0, blocking collectives: 278 us -> none  [the longest x4 228 us: shards(): lax.psum(jnp.dot(select, weights, precision=lax.Precision.HIGHEST), 'tgt')]
    reduce_scatter x1 -> x0, waiting for transfers between devices: 202 us -> none  [shards(): return lax.psum_scatter(contrib, 'tgt', scatter_dimension=0, tiled=True)]
    pallas_call x0 -> x1, Pallas kernels: none -> 139 us  [shards(): pl.pallas_call(sinkhorn_kernel, out_shape=jax.ShapeDtypeStruct((8, BLK),...]
    all_gather x2 -> x0, waiting for transfers between devices: 67.8 us -> none  [the longest x1 67.8 us: shards(): group_h = lax.all_gather(own_h, 'tgt', axis=0, tiled=True)]
  transfers between devices with their start and end apart: 3 -> 0, of which waited for: 2 -> 0; matrix products, arithmetic and copies ran while one was open for 22% -> 0% of each run, Pallas kernels for 0% -> 0%
where the time goes in v1:
time: 145 us; the launch traced here: 144 us
  Pallas kernels  139 us (96%)
  local copies, waits for them, and re-layouts  4.75 us (3%)
    pallas_call x1, Pallas kernels, shards(): pl.pallas_call(sinkhorn_kernel, out_shape=jax.ShapeDtypeStruct((8, BLK),...  139 us
    unnamed x20, local copies, waits for them, and re-layouts  3.88 us

profile of v1, /device:TPU:1, one launch (start us, length us, event | category | flops | bytes accessed | tf_op | source)
XLA Modules:
  0.0 144.5 jit_solution(54705285768276582)
XLA Ops:
  0.0 0.0 copy-start
  0.0 0.0 copy-start.8
  0.0 0.0 copy-start.9
  0.0 0.7 copy-done.8
  0.7 0.0 copy-done.9
  0.7 0.0 copy-start.6
  0.7 0.1 pad_add_fusion.sl_ref
  0.8 0.6 copy-done.6
  1.4 0.4 fusion
  1.8 0.1 copy.14
  1.9 0.4 convert_reduce_fusion
  2.3 0.1 select_reduce_fusion
  2.4 0.0 copy-start.5
  2.4 0.1 select_reduce_fusion.1
  2.5 0.0 copy-start.7
  2.5 0.1 select_n.34.place_ref
  2.6 0.5 copy-done.5
  3.1 0.1 copy-done.7
  3.2 0.0 copy-start.4
  3.2 0.0 copy-done
  3.2 0.0 copy-start.2
  3.2 0.0 copy-start.3
  3.3 0.7 copy-done.4
  4.0 0.2 copy-done.2
  4.1 0.1 copy-done.3
  4.2 0.0 copy-start.1
  4.2 1.0 copy-done.1
  5.2 138.6 %shard_map.100 = f32[8,128]{1,0:T(8,128)S(1)} custom-call(s32[32]{0:T(128)S(1)} %broadcast_add_fusion.2.srow_ref, s32[128]{0:T(128)S(1)} %select_n.34.place_ref, bf16[64,256]{1,0:T(8,128)(2,1)S(1)} %copy-done.4, s32[8,128]{1,0:T(8,128)S(1)} %pad_add_fusion.sl_ref, bf16[1024,256]{1,0:T(8,128)(2,1)S(1)} %copy-done.1, s32[8,1024]{1,0:T(8,128)S(1)} %select_bitcast_fusion.tl_ref, ...), custom_call_target="tpu_custom_call" | custom-call | tf_op jit(solution)/shard_map/pallas_call | solution.py:427
  143.8 0.1 reshape.85
  143.9 0.6 copy.20
  (11 shorter events, 0.1 us)
Async XLA Ops:
  0.0 3.2 %copy-start = (s32[2048,16]{0,1:T(8,128)S(1)}, s32[2048,16]{0,1:T(8,128)}, u32[]{:S(2)}) copy-start(s32[2048,16]{0,1:T(8,128)} %param.19) | copy-start | bytes 393220
  0.0 0.7 copy-start.8
  0.0 0.7 copy-start.9
  0.7 0.7 copy-start.6
  2.4 0.8 copy-start.5
  2.5 0.7 copy-start.7
  3.2 0.8 copy-start.4
  3.2 0.9 copy-start.2
  3.2 1.0 copy-start.3
  4.2 1.0 copy-start.1

commit v2 on v1

v2 whole, which is shorter than its diff:
```python
import functools
import math

import jax
import jax.numpy as jnp
from jax import lax
from jax.experimental import pallas as pl
from jax.experimental.pallas import tpu as pltpu
from jax.sharding import PartitionSpec as P

D = 256
BLK = 128
CAND = 32
MOST = 4
QRY = 16
SWEEPS = 4
KMAX = 8
NY, NZ = 4, 8
NSRC, NTGT = 8, 32
ROWS = 64
R_BLK = 16
C_LOC = 8
SLOTS = C_LOC * MOST
A_ROWS = 48
B_ROWS = 16
WIDE = 256
NEG = -1e30
FLOOR = -1e29
SCALE = 3.0 / math.sqrt(D)
MESH = pl.DeviceIdType.MESH
BF = jnp.bfloat16
F32 = jnp.float32


def far_first():
    offs = [(dy, dz) for dy in range(NY) for dz in range(NZ) if (dy, dz) != (0, 0)]
    dist = lambda o: min(o[0], NY - o[0]) + min(o[1], NZ - o[1])
    return sorted(offs, key=lambda o: (-dist(o), o))


Z_FAR = (4, 3, 5, 2, 6, 1, 7)
Z_NEAR = (1, 7, 2, 6, 3, 5, 4)
Y_FAR = (2, 1, 3)


def sinkhorn_kernel(
    x_hbm, sl_hbm, sd_hbm, t_hbm, tl_hbm, td_hbm, ws_hbm, wn_hbm, cand_hbm, pp_hbm,
    out_ref,
    sl_ref, sd_ref, t_ref, tl_ref, td_ref, ws_ref, wn_ref, cand_ref, pq_ref,
    tab_ref, pp_ref, meta_ref, meta_s, acc_ref, in_sem, meta_sem,
    iota_ref, big_x, xt_ref, lk_ref, at_ref, ht_ref, tt_ref, att_ref, th_ref,
    s_ref, e_ref, wb_ref, rx_ref, rh_ref, cx_ref, top_ref, r0_ref, u_ref, sid_ref, g_ref, pk_ref,
    fs_ref, fr_ref,
    a_send, a_recv, b_send, b_recv, ya_send, ya_recv, zb_send, zb_recv, lk_send, lk_recv,
    r_send, r_recv, c_send, c_recv, f_send, f_recv,
):
    s = lax.axis_index("src")
    t = lax.axis_index("tgt")
    y = t // NZ
    z = lax.rem(t, NZ)
    tgt_peers = [lax.rem(y + dy, NY) * NZ + lax.rem(z + dz, NZ) for dy, dz in far_first()]
    sx = s // 2
    score = lax.rem(s, 2)
    src_peers = [
        lax.rem(sx + dx, 4) * 2 + (score if same else 1 - score)
        for dx, same in ((2, False), (2, True), (1, False), (3, False), (1, True), (3, True), (0, False))
    ]

    staged = (
        (sl_hbm, sl_ref), (sd_hbm, sd_ref), (cand_hbm, cand_ref), (tl_hbm, tl_ref), (td_hbm, td_ref),
        (t_hbm, t_ref), (ws_hbm, ws_ref), (wn_hbm, wn_ref), (pp_hbm, pq_ref),
        (x_hbm, big_x.at[pl.ds(t * ROWS, ROWS)]),
    )
    loads = [pltpu.make_async_copy(src, dst, in_sem.at[i]) for i, (src, dst) in enumerate(staged)]
    for load in loads:
        load.start()

    barrier = pltpu.get_barrier_semaphore()
    for p in tgt_peers:
        pl.semaphore_signal(barrier, inc=1, device_id=(s, p), device_id_type=MESH)
    for p in src_peers:
        pl.semaphore_signal(barrier, inc=1, device_id=(p, t), device_id_type=MESH)

    tile_rows = lax.broadcasted_iota(jnp.int32, (WIDE // 16, 16, BLK), 0) * 16
    tile_rows = tile_rows + lax.broadcasted_iota(jnp.int32, (WIDE // 16, 16, BLK), 1)
    iota_ref[...] = tile_rows.astype(jnp.int16)
    lane4 = lax.broadcasted_iota(jnp.int32, (KMAX // 2, BLK), 1)
    loads[0].wait()
    loads[1].wait()
    slot8 = lax.broadcasted_iota(jnp.int32, (KMAX, ROWS), 0)
    own = jnp.where(slot8 < sd_ref[...], sl_ref[...], -1)
    own = jnp.concatenate([own, own], axis=1)
    lk_ref[t] = jnp.where(lane4 < ROWS, own[:4], own[4:])

    loads[2].wait()
    local = cand_ref[...] - t * C_LOC
    local = jnp.concatenate([local, jnp.full((R_BLK, BLK - CAND), -1, jnp.int32)], axis=1)
    lane16 = lax.broadcasted_iota(jnp.int32, (R_BLK, BLK), 1)
    row16 = lax.broadcasted_iota(jnp.int32, (R_BLK, BLK), 0)
    hits = jnp.zeros((R_BLK, BLK), jnp.int32)
    for c in range(C_LOC):
        named = jnp.max(jnp.where(local == c, 1, 0), axis=1, keepdims=True)
        hits = jnp.where(lane16 == c, named, hits)
    before = jnp.zeros((R_BLK, BLK), jnp.int32)
    for r in range(R_BLK - 1):
        before = before + jnp.where(row16 > r, hits[r : r + 1, :], 0)
    place = jnp.where(hits > 0, lane16 * MOST + before, SLOTS)
    meta_ref[:R_BLK, :] = place
    rows_of_slot = [
        jnp.sum(
            jnp.where((hits > 0) & (before == m), row16 + 1, 0), axis=0, keepdims=True
        )
        for m in range(MOST)
    ]
    pad4 = jnp.zeros((8 - MOST, BLK), jnp.int32)
    meta_ref[R_BLK:, :] = jnp.concatenate(rows_of_slot + [pad4], axis=0) - 1
    table = jnp.full((R_BLK, BLK), -1, jnp.int32)
    for c in range(C_LOC):
        table = jnp.where(local == c, jnp.broadcast_to(place[:, c : c + 1], (R_BLK, BLK)), table)
    tab_ref[...] = table
    to_scalar = pltpu.make_async_copy(meta_ref, meta_s, meta_sem)
    to_scalar.start()

    def row_of(c, m):
        return meta_s[R_BLK + m, c]

    def row_at(c, m):
        return jnp.clip(row_of(c, m), 0, R_BLK - 1)

    g_ref[SLOTS] = jnp.zeros((QRY, BLK), F32)

    for load in loads[3:]:
        load.wait()
    for block in range(R_BLK):
        pp_ref[block] = pq_ref[:, block * BLK : (block + 1) * BLK]
    ws_t = ws_ref[...].T
    wn_t = wn_ref[...].T
    for chunk in range(4):
        tt_ref[:, chunk * WIDE : (chunk + 1) * WIDE] = t_ref[chunk * WIDE : (chunk + 1) * WIDE, :].T

    def build(links, chunks, put):
        singles = [part[k : k + 1, :] for part in links for k in range(part.shape[0])]
        rows, counts = [], []
        for part in links:
            count = jnp.zeros(part.shape, F32)
            for single in singles:
                count = count + jnp.where(part == single, 1.0, 0.0)
            counts += [
                jnp.broadcast_to(count[k : k + 1, :], (16, BLK)).astype(BF) for k in range(part.shape[0])
            ]
        for single in singles:
            rows.append(jnp.broadcast_to(single, (16, BLK)).astype(jnp.int16))

        def body(q, _):
            base = jnp.full((16, BLK), q * WIDE, jnp.int32).astype(jnp.int16)
            total = jnp.zeros((WIDE // 16, 16, BLK), BF)
            for k in range(KMAX):
                total = jnp.where((rows[k] - base)[None] == iota_ref[...], counts[k][None], total)
            put(q, total.reshape(WIDE, BLK))
            return 0

        lax.fori_loop(0, chunks, body, 0)

    def encode(table_t, adjacency, own_t, degree):
        total = jnp.dot(table_t, adjacency, preferred_element_type=F32)
        mean = (total / degree).astype(BF)
        mixed = jnp.dot(ws_t, own_t, preferred_element_type=F32) + jnp.dot(
            wn_t, mean, preferred_element_type=F32
        )
        return mixed.astype(BF)

    for chunk in range(4):
        cols = slice(chunk * WIDE, (chunk + 1) * WIDE)
        degree = td_ref[:, cols]
        slot_rows = lax.broadcasted_iota(jnp.int32, (KMAX, WIDE), 0)
        links = jnp.where(slot_rows < degree, tl_ref[:, cols], -1)
        degree = degree.astype(F32)
        for half in range(2):
            def put(q, value, half=half):
                att_ref[pl.ds(q * WIDE, WIDE), half * BLK : (half + 1) * BLK] = value

            build([links[:, half * BLK : (half + 1) * BLK]], 4, put)
        coded = encode(tt_ref[...], att_ref[...], tt_ref[:, cols], degree).T
        th_ref[2 * chunk] = coded[:BLK]
        th_ref[2 * chunk + 1] = coded[BLK:]

    pl.semaphore_wait(barrier, NTGT - 1 + NSRC - 1)

    def push(src, dst, ssem, rsem, dev):
        pltpu.make_async_remote_copy(
            src_ref=src, dst_ref=dst, send_sem=ssem, recv_sem=rsem, device_id=dev, device_id_type=MESH
        ).start()

    def drain(ref, sem):
        pltpu.make_async_copy(ref, ref, sem).wait()

    def part_a(d):
        return big_x.at[pl.ds(d * ROWS, A_ROWS)]

    def part_b(d):
        return big_x.at[pl.ds(d * ROWS + A_ROWS, B_ROWS)]

    def at_yz(dy, dz):
        return lax.rem(y + dy + NY, NY) * NZ + lax.rem(z + dz + NZ, NZ)

    for k in Z_FAR:
        push(part_a(t), part_a(t), a_send, a_recv.at[k], (s, at_yz(0, k)))
    for j in Y_FAR:
        push(part_b(t), part_b(t), b_send, b_recv.at[j], (s, at_yz(j, 0)))
    for p in tgt_peers:
        push(lk_ref.at[t], lk_ref.at[t], lk_send, lk_recv, (s, p))
    for j in Y_FAR:
        push(part_a(t), part_a(t), ya_send, ya_recv.at[j], (s, at_yz(j, 0)))
    for k in Z_FAR:
        push(part_b(t), part_b(t), zb_send, zb_recv.at[0], (s, at_yz(0, k)))

    for j in Y_FAR[::-1]:
        drain(part_b(t), b_recv.at[j])
        d = at_yz(-j, 0)
        for k in Z_FAR:
            push(part_b(d), part_b(d), zb_send, zb_recv.at[j], (s, at_yz(0, k)))
    for k in Z_NEAR:
        drain(part_a(t), a_recv.at[k])
        d = at_yz(0, -k)
        for j in Y_FAR:
            push(part_a(d), part_a(d), ya_send, ya_recv.at[j], (s, at_yz(j, 0)))

    drain(lk_ref.at[pl.ds(0, NTGT - 1)], lk_recv)

    def group_links(block):
        first, second = lk_ref[2 * block], lk_ref[2 * block + 1]
        return [
            jnp.where(lane4 < ROWS, first, pltpu.roll(second, ROWS, 1)),
            jnp.where(lane4 < ROWS, pltpu.roll(first, ROWS, 1), second),
        ]

    def build_pair(pair, _):
        for half in range(2):
            def put(q, value, half=half):
                at_ref[pair, pl.ds(q * WIDE, WIDE), half * BLK : (half + 1) * BLK] = value

            build(group_links(2 * pair + half), 8, put)
        return 0

    lax.fori_loop(0, 8, build_pair, 0)

    for step, j in enumerate((0, 1, 3, 2)):
        if j:
            drain(big_x.at[pl.ds(0, NZ * A_ROWS)], ya_recv.at[j])
        drain(big_x.at[pl.ds(0, (NZ - 1) * B_ROWS)], zb_recv.at[j])
        pair_base = lax.rem(y - j + NY, NY) * 2
        for h in range(2):
            q = pair_base + h
            xt_ref[q] = big_x[pl.ds(pl.multiple_of(q * WIDE, WIDE), WIDE), :].T

        def add_pair(pair, _):
            total = None if step == 0 else acc_ref[pair]
            for h in range(2):
                q = pair_base + h
                part = jnp.dot(
                    xt_ref[q], at_ref[pair, pl.ds(pl.multiple_of(q * WIDE, WIDE), WIDE), :],
                    preferred_element_type=F32,
                )
                total = part if total is None else total + part
            if step < NY - 1:
                acc_ref[pair] = total
                return 0
            links = [
                jnp.concatenate(parts, axis=1)
                for parts in zip(group_links(2 * pair), group_links(2 * pair + 1))
            ]
            degree = sum(jnp.sum((part >= 0).astype(F32), axis=0, keepdims=True) for part in links)
            mean = (total / degree).astype(BF)
            mixed = jnp.dot(ws_t, xt_ref[pair], preferred_element_type=F32) + jnp.dot(
                wn_t, mean, preferred_element_type=F32
            )
            coded = mixed.astype(BF)
            ht_ref[2 * pair] = coded[:, :BLK]
            ht_ref[2 * pair + 1] = coded[:, BLK:]
            return 0

        lax.fori_loop(0, 8, add_pair, 0)

    to_scalar.wait()
    block_id = lax.broadcasted_iota(jnp.int32, (R_BLK, BLK), 0)
    lane = lax.broadcasted_iota(jnp.int32, (BLK, BLK), 1)
    neg16 = jnp.full((R_BLK, BLK), NEG, F32)

    def score_block(c, best):
        for m in range(MOST):
            r = row_of(c, m)
            bias = jnp.where(r < 0, NEG, 0.0)
            raw = jnp.dot(th_ref[c], ht_ref[row_at(c, m)], preferred_element_type=F32)
            raw = raw * SCALE + bias
            s_ref[c * MOST + m] = raw
            best = jnp.maximum(best, jnp.where(block_id == r, jnp.max(raw, axis=0, keepdims=True), NEG))
        return best

    top = lax.fori_loop(0, C_LOC, score_block, neg16)
    top_ref[...] = top

    def first_rows(c, total):
        for m in range(MOST):
            r = row_of(c, m)
            high = top_ref[pl.ds(row_at(c, m), 1), :]
            part = jnp.sum(jnp.exp(s_ref[c * MOST + m] - high), axis=0, keepdims=True)
            total = total + jnp.where(block_id == r, part, 0.0)
        return total

    total = lax.fori_loop(0, C_LOC, first_rows, jnp.zeros((R_BLK, BLK), F32))
    rx_ref[0, t] = jnp.where(total > 0.0, top + jnp.log(total), NEG)

    def send_rows(sweep, buf, slot):
        for p in tgt_peers:
            push(buf.at[slot, t], buf.at[slot, t], r_send.at[sweep], r_recv.at[sweep], (s, p))

    def await_rows(sweep, buf, slot):
        drain(buf.at[slot, pl.ds(0, NTGT - 1)], r_recv.at[sweep])
        return buf[slot]

    def send_cols(sweep):
        for p in src_peers:
            push(cx_ref.at[sweep, s], cx_ref.at[sweep, s], c_send.at[sweep], c_recv.at[sweep], (p, t))

    def await_cols(sweep):
        drain(cx_ref.at[sweep, pl.ds(0, NSRC - 1)], c_recv.at[sweep])
        return cx_ref[sweep]

    send_rows(0, rx_ref, 0)

    def probe_slots(block, _):
        table = jnp.broadcast_to(tab_ref[pl.ds(block, 1), :], (8, BLK))
        for half in range(2):
            rows = slice(half * 8, half * 8 + 8)
            which = pp_ref[block, rows, :] // BLK
            sid_ref[block, rows, :] = jnp.take_along_axis(table, which, axis=1)
        return 0

    lax.fori_loop(0, R_BLK, probe_slots, 0)

    def pick(slot, _):
        r = row_at(slot // MOST, lax.rem(slot, MOST))
        for half in range(2):
            rows = slice(half * 8, half * 8 + 8)
            offset = lax.rem(pp_ref[r, rows, :], BLK)
            strip, inner = offset // 8, lax.rem(offset, 8)
            value = jnp.zeros((8, BLK), F32)
            for k in range(BLK // 8):
                got = jnp.take_along_axis(s_ref[slot, k * 8 : k * 8 + 8, :], inner, axis=0)
                value = jnp.where(strip == k, got, value)
            g_ref[slot, rows, :] = jnp.where(sid_ref[r, rows, :] == slot, value, 0.0)
        return 0

    lax.fori_loop(0, SLOTS, pick, 0)

    def merge(block, _):
        total = jnp.zeros((QRY, BLK), F32)
        for c in range(C_LOC):
            total = total + g_ref[jnp.clip(meta_s[block, c], 0, SLOTS)]
        pk_ref[block] = total
        return 0

    lax.fori_loop(0, R_BLK, merge, 0)

    parts = await_rows(0, rx_ref, 0)
    high = jnp.max(parts, axis=0)
    r0 = -(high + jnp.log(jnp.sum(jnp.exp(parts - high[None]), axis=0)))
    r0_ref[...] = r0

    def first_cols(c, carry):
        tops, sums = carry
        shifted = [
            s_ref[c * MOST + m] + r0_ref[pl.ds(row_at(c, m), 1), :]
            for m in range(MOST)
        ]
        high = functools.reduce(jnp.maximum, shifted)
        high = jnp.maximum(jnp.max(high, axis=1, keepdims=True), FLOOR)
        total = jnp.zeros((BLK, BLK), F32)
        for m in range(MOST):
            e = jnp.exp(shifted[m] - high)
            e_ref[c * MOST + m] = e
            total = total + e
        total = jnp.sum(total, axis=1, keepdims=True)
        return jnp.where(lane == c, high, tops), jnp.where(lane == c, total, sums)

    zero_tile = jnp.zeros((BLK, BLK), F32)
    tops, sums = lax.fori_loop(0, C_LOC, first_cols, (zero_tile, zero_tile))
    tops = tops.T[:C_LOC]
    sums = sums.T[:C_LOC]
    cx_ref[0, s] = jnp.where(sums > 0.0, tops + jnp.log(sums), NEG)
    send_cols(0)
    parts = await_cols(0)
    high = jnp.max(parts, axis=0)
    share = R_BLK * BLK * NSRC / (C_LOC * BLK * NTGT)
    c0 = math.log(share) - (high + jnp.log(jnp.sum(jnp.exp(parts - high[None]), axis=0)))
    factor = jnp.exp(tops + c0)

    def spread(weights):
        upright = jnp.concatenate([weights, jnp.zeros((BLK - C_LOC, BLK), F32)], axis=0).T
        for c in range(C_LOC):
            wb_ref[c] = jnp.broadcast_to(upright[:, c : c + 1], (BLK, BLK))

    def sweep_body(sweep, carry, rows_buf):
        _, col_scale = carry
        spread(factor * col_scale)

        def rows_of(c, total):
            for m in range(MOST):
                part = jnp.sum(e_ref[c * MOST + m] * wb_ref[c], axis=0, keepdims=True)
                total = total + jnp.where(block_id == row_of(c, m), part, 0.0)
            return total

        total = lax.fori_loop(0, C_LOC, rows_of, jnp.zeros((R_BLK, BLK), F32))
        slot = 1 if rows_buf is rx_ref else sweep - 1
        rows_buf[slot, t] = total.astype(rows_buf.dtype)
        send_rows(sweep, rows_buf, slot)
        parts = await_rows(sweep, rows_buf, slot)
        row_scale = 1.0 / jnp.sum(parts.astype(F32), axis=0)
        u_ref[...] = row_scale

        def cols_of(c, sums):
            total = jnp.zeros((BLK, BLK), F32)
            for m in range(MOST):
                r = row_at(c, m)
                total = total + e_ref[c * MOST + m] * u_ref[pl.ds(r, 1), :]
            return jnp.where(lane == c, jnp.sum(total, axis=1, keepdims=True), sums)

        sums = lax.fori_loop(0, C_LOC, cols_of, zero_tile).T[:C_LOC]
        cx_ref[sweep, s] = sums * factor
        send_cols(sweep)
        return row_scale, share / jnp.sum(await_cols(sweep), axis=0)

    scales = (jnp.ones((R_BLK, BLK), F32), jnp.ones((C_LOC, BLK), F32))
    scales = lax.fori_loop(1, SWEEPS - 1, lambda i, carry: sweep_body(i, carry, rh_ref), scales)
    row_scale, col_scale = sweep_body(SWEEPS - 1, scales, rx_ref)
    row_pot = r0 + jnp.log(row_scale)
    col_pot = c0 + jnp.log(col_scale) + math.log(CAND * BLK)
    u_ref[...] = row_pot
    top_ref[:C_LOC, :] = col_pot
    lane8 = lax.broadcasted_iota(jnp.int32, (8, BLK), 1)

    def finish(block, _):
        done = []
        for half in range(2):
            rows = slice(half * 8, half * 8 + 8)
            sid = sid_ref[block, rows, :]
            offset = lax.rem(pp_ref[block, rows, :], BLK)
            owner = sid // MOST
            value = jnp.zeros((8, BLK), F32)
            for c in range(C_LOC):
                strip = jnp.broadcast_to(top_ref[c : c + 1, :], (8, BLK))
                value = jnp.where(owner == c, jnp.take_along_axis(strip, offset, axis=1), value)
            value = value + pk_ref[block, rows, :] + u_ref[pl.ds(block, 1), :]
            done.append(jnp.where(sid >= 0, value, 0.0))
        low, high = done
        fs_ref[2 * block] = jnp.where(lane8 < ROWS, low, pltpu.roll(high, ROWS, 1))
        fs_ref[2 * block + 1] = jnp.where(lane8 < ROWS, pltpu.roll(low, ROWS, 1), high)
        return 0

    lax.fori_loop(0, R_BLK, finish, 0)
    for p in tgt_peers:
        push(fs_ref.at[p], fr_ref.at[t], f_send, f_recv, (s, p))
    fr_ref[t] = fs_ref[t]
    drain(fr_ref.at[pl.ds(0, NTGT - 1)], f_recv)
    out_ref[...] = jnp.sum(fr_ref[...], axis=0)

    drain(big_x.at[pl.ds(0, 7 * A_ROWS)], a_send)
    drain(big_x.at[pl.ds(0, 3 * B_ROWS)], b_send)
    drain(big_x.at[pl.ds(0, 24 * A_ROWS)], ya_send)
    drain(big_x.at[pl.ds(0, 28 * B_ROWS)], zb_send)
    drain(lk_ref.at[pl.ds(0, NTGT - 1)], lk_send)
    for sweep in range(SWEEPS):
        rows_sent = rh_ref.at[sweep - 1] if 0 < sweep < SWEEPS - 1 else rx_ref.at[min(sweep, 1)]
        drain(rows_sent.at[pl.ds(0, NTGT - 1)], r_send.at[sweep])
        drain(cx_ref.at[sweep, pl.ds(0, NSRC - 1)], c_send.at[sweep])
    drain(fs_ref.at[pl.ds(0, NTGT - 1)], f_send)


def shards(
    source_embed,
    source_links,
    source_degree,
    target_embed,
    target_links,
    target_degree,
    w_self,
    w_neigh,
    cand_blocks,
    probe_pairs,
):
    vmem = pl.BlockSpec(memory_space=pltpu.VMEM)
    hbm = pl.BlockSpec(memory_space=pltpu.HBM)
    dma = pltpu.SemaphoreType.DMA
    packed = pl.pallas_call(
        sinkhorn_kernel,
        out_shape=jax.ShapeDtypeStruct((8, BLK), F32),
        in_specs=[hbm] * 10,
        out_specs=vmem,
        scratch_shapes=[
            pltpu.VMEM((KMAX, ROWS), jnp.int32),
            pltpu.VMEM((1, ROWS), jnp.int32),
            pltpu.VMEM((C_LOC * BLK, D), BF),
            pltpu.VMEM((KMAX, C_LOC * BLK), jnp.int32),
            pltpu.VMEM((1, C_LOC * BLK), jnp.int32),
            pltpu.VMEM((D, D), BF),
            pltpu.VMEM((D, D), BF),
            pltpu.VMEM((R_BLK, CAND), jnp.int32),
            pltpu.VMEM((QRY, R_BLK * BLK), jnp.int32),
            pltpu.VMEM((R_BLK, BLK), jnp.int32),
            pltpu.VMEM((R_BLK, QRY, BLK), jnp.int32),
            pltpu.VMEM((R_BLK + 8, BLK), jnp.int32),
            pltpu.SMEM((R_BLK + 8, BLK), jnp.int32),
            pltpu.VMEM((8, D, WIDE), F32),
            dma((10,)),
            dma,
            pltpu.VMEM((WIDE // 16, 16, BLK), jnp.int16),
            pltpu.VMEM((NTGT * ROWS, D), BF),
            pltpu.VMEM((8, D, WIDE), BF),
            pltpu.VMEM((NTGT, KMAX // 2, BLK), jnp.int32),
            pltpu.VMEM((8, NTGT * ROWS, WIDE), BF),
            pltpu.VMEM((R_BLK, D, BLK), BF),
            pltpu.VMEM((D, C_LOC * BLK), BF),
            pltpu.VMEM((C_LOC * BLK, WIDE), BF),
            pltpu.VMEM((C_LOC, BLK, D), BF),
            pltpu.VMEM((SLOTS, BLK, BLK), F32),
            pltpu.VMEM((SLOTS, BLK, BLK), F32),
            pltpu.VMEM((C_LOC, BLK, BLK), F32),
            pltpu.VMEM((2, NTGT, R_BLK, BLK), F32),
            pltpu.VMEM((SWEEPS - 2, NTGT, R_BLK, BLK), BF),
            pltpu.VMEM((SWEEPS, NSRC, C_LOC, BLK), F32),
            pltpu.VMEM((R_BLK, BLK), F32),
            pltpu.VMEM((R_BLK, BLK), F32),
            pltpu.VMEM((R_BLK, BLK), F32),
            pltpu.VMEM((R_BLK, QRY, BLK), jnp.int32),
            pltpu.VMEM((SLOTS + 1, QRY, BLK), F32),
            pltpu.VMEM((R_BLK, QRY, BLK), F32),
            pltpu.VMEM((NTGT, 8, BLK), F32),
            pltpu.VMEM((NTGT, 8, BLK), F32),
            dma, dma((NZ,)), dma, dma((NY,)), dma, dma((NY,)), dma, dma((NY,)), dma, dma,
            dma((SWEEPS,)), dma((SWEEPS,)), dma((SWEEPS,)), dma((SWEEPS,)), dma, dma,
        ],
        compiler_params=pltpu.CompilerParams(
            collective_id=0, has_side_effects=True, vmem_limit_bytes=64 * 2**20
        ),
    )(
        source_embed, source_links.T, source_degree.reshape(1, -1), target_embed, target_links.T,
        target_degree.reshape(1, -1), w_self, w_neigh, cand_blocks, probe_pairs.T,
    )
    return packed.reshape(8, 2, ROWS).transpose(2, 1, 0).reshape(ROWS, QRY)


def solution(mesh):
    placed = (
        P(("src", "tgt"), None),
        P(("src", "tgt"), None),
        P(("src", "tgt")),
        P("tgt", None),
        P("tgt", None),
        P("tgt"),
        P(),
        P(),
        P("src", None),
        P("src", None),
    )
    return jax.shard_map(
        shards, mesh=mesh, in_specs=placed, out_specs=P(("src", "tgt"), None), check_vma=False
    )
```

time: 145 us -> 102 us (0.70)
  Pallas kernels: 139 us -> 101 us
  local copies, waits for them, and re-layouts: 4.75 us -> 1.36 us
    pallas_call x1, Pallas kernels: 139 us -> 101 us  [shards(): pl.pallas_call(sinkhorn_kernel, out_shape=jax.ShapeDtypeStruct((8, BLK),...]
    unnamed x20 -> x0, local copies, waits for them, and re-layouts: 3.88 us -> none
where the time goes in v2:
time: 102 us
  Pallas kernels  101 us (99%)
  local copies, waits for them, and re-layouts  1.36 us (1%)
    pallas_call x1, Pallas kernels, shards(): pl.pallas_call(sinkhorn_kernel, out_shape=jax.ShapeDtypeStruct((8, BLK),...  101 us

profile of v2, /device:TPU:1, one launch (start us, length us, event | category | flops | bytes accessed | tf_op | source)
XLA Modules:
  0.0 102.2 jit_solution(12596925173900010679)
XLA Ops:
  0.0 100.8 %shard_map.100 = f32[8,128]{1,0:T(8,128)} custom-call(bf16[64,256]{1,0:T(8,128)(2,1)} %x_hbm.1, s32[8,64]{1,0:T(8,128)} %bitcast.12, s32[1,64]{1,0:T(1,128)} %bitcast.14, bf16[1024,256]{1,0:T(8,128)(2,1)} %t_hbm.1, s32[8,1024]{1,0:T(8,128)} %bitcast.10, s32[1,1024]{1,0:T(1,128)} %bitcast.13, bf16[256,256]{1,0:T(8,128)(2,1)} %ws_hbm.1, ...), custom_call_target="tpu_custom_call" | custom-call | tf_op jit(solution)/shard_map/pallas_call | solution.py:494
  100.8 0.8 reshape.14
  101.6 0.6 copy.13

commit v3 on v2

--- a/solution.py
+++ b/solution.py
@@ -203,12 +203,12 @@
     def at_yz(dy, dz):
         return lax.rem(y + dy + NY, NY) * NZ + lax.rem(z + dz + NZ, NZ)
 
+    for p in tgt_peers:
+        push(lk_ref.at[t], lk_ref.at[t], lk_send, lk_recv, (s, p))
     for k in Z_FAR:
         push(part_a(t), part_a(t), a_send, a_recv.at[k], (s, at_yz(0, k)))
     for j in Y_FAR:
         push(part_b(t), part_b(t), b_send, b_recv.at[j], (s, at_yz(j, 0)))
-    for p in tgt_peers:
-        push(lk_ref.at[t], lk_ref.at[t], lk_send, lk_recv, (s, p))
     for j in Y_FAR:
         push(part_a(t), part_a(t), ya_send, ya_recv.at[j], (s, at_yz(j, 0)))
     for k in Z_FAR:
@@ -219,12 +219,14 @@
         d = at_yz(-j, 0)
         for k in Z_FAR:
             push(part_b(d), part_b(d), zb_send, zb_recv.at[j], (s, at_yz(0, k)))
-    for k in Z_NEAR:
-        drain(part_a(t), a_recv.at[k])
-        d = at_yz(0, -k)
-        for j in Y_FAR:
-            push(part_a(d), part_a(d), ya_send, ya_recv.at[j], (s, at_yz(j, 0)))
-
+    def relay(near):
+        for k in near:
+            drain(part_a(t), a_recv.at[k])
+            d = at_yz(0, -k)
+            for j in Y_FAR:
+                push(part_a(d), part_a(d), ya_send, ya_recv.at[j], (s, at_yz(j, 0)))
+
+    relay(Z_NEAR[:4])
     drain(lk_ref.at[pl.ds(0, NTGT - 1)], lk_recv)
 
     def group_links(block):
@@ -242,7 +244,11 @@
             build(group_links(2 * pair + half), 8, put)
         return 0
 
-    lax.fori_loop(0, 8, build_pair, 0)
+    lax.fori_loop(0, 2, build_pair, 0)
+    relay(Z_NEAR[4:6])
+    lax.fori_loop(2, 4, build_pair, 0)
+    relay(Z_NEAR[6:])
+    lax.fori_loop(4, 8, build_pair, 0)
 
     for step, j in enumerate((0, 1, 3, 2)):
         if j:
@@ -296,7 +302,7 @@
             best = jnp.maximum(best, jnp.where(block_id == r, jnp.max(raw, axis=0, keepdims=True), NEG))
         return best
 
-    top = lax.fori_loop(0, C_LOC, score_block, neg16)
+    top = lax.fori_loop(0, C_LOC, score_block, neg16, unroll=2)
     top_ref[...] = top
 
     def first_rows(c, total):
@@ -307,7 +313,7 @@
             total = total + jnp.where(block_id == r, part, 0.0)
         return total
 
-    total = lax.fori_loop(0, C_LOC, first_rows, jnp.zeros((R_BLK, BLK), F32))
+    total = lax.fori_loop(0, C_LOC, first_rows, jnp.zeros((R_BLK, BLK), F32), unroll=4)
     rx_ref[0, t] = jnp.where(total > 0.0, top + jnp.log(total), NEG)
 
     def send_rows(sweep, buf, slot):
@@ -351,7 +357,7 @@
             g_ref[slot, rows, :] = jnp.where(sid_ref[r, rows, :] == slot, value, 0.0)
         return 0
 
-    lax.fori_loop(0, SLOTS, pick, 0)
+    lax.fori_loop(0, SLOTS, pick, 0, unroll=2)
 
     def merge(block, _):
         total = jnp.zeros((QRY, BLK), F32)
@@ -360,7 +366,7 @@
         pk_ref[block] = total
         return 0
 
-    lax.fori_loop(0, R_BLK, merge, 0)
+    lax.fori_loop(0, R_BLK, merge, 0, unroll=4)
 
     parts = await_rows(0, rx_ref, 0)
     high = jnp.max(parts, axis=0)
@@ -384,7 +390,7 @@
         return jnp.where(lane == c, high, tops), jnp.where(lane == c, total, sums)
 
     zero_tile = jnp.zeros((BLK, BLK), F32)
-    tops, sums = lax.fori_loop(0, C_LOC, first_cols, (zero_tile, zero_tile))
+    tops, sums = lax.fori_loop(0, C_LOC, first_cols, (zero_tile, zero_tile), unroll=2)
     tops = tops.T[:C_LOC]
     sums = sums.T[:C_LOC]
     cx_ref[0, s] = jnp.where(sums > 0.0, tops + jnp.log(sums), NEG)
@@ -410,7 +416,7 @@
                 total = total + jnp.where(block_id == row_of(c, m), part, 0.0)
             return total
 
-        total = lax.fori_loop(0, C_LOC, rows_of, jnp.zeros((R_BLK, BLK), F32))
+        total = lax.fori_loop(0, C_LOC, rows_of, jnp.zeros((R_BLK, BLK), F32), unroll=4)
         slot = 1 if rows_buf is rx_ref else sweep - 1
         rows_buf[slot, t] = total.astype(rows_buf.dtype)
         send_rows(sweep, rows_buf, slot)
@@ -425,7 +431,7 @@
                 total = total + e_ref[c * MOST + m] * u_ref[pl.ds(r, 1), :]
             return jnp.where(lane == c, jnp.sum(total, axis=1, keepdims=True), sums)
 
-        sums = lax.fori_loop(0, C_LOC, cols_of, zero_tile).T[:C_LOC]
+        sums = lax.fori_loop(0, C_LOC, cols_of, zero_tile, unroll=4).T[:C_LOC]
         cx_ref[sweep, s] = sums * factor
         send_cols(sweep)
         return row_scale, share / jnp.sum(await_cols(sweep), axis=0)
@@ -457,7 +463,7 @@
         fs_ref[2 * block + 1] = jnp.where(lane8 < ROWS, pltpu.roll(low, ROWS, 1), high)
         return 0
 
-    lax.fori_loop(0, R_BLK, finish, 0)
+    lax.fori_loop(0, R_BLK, finish, 0, unroll=4)
     for p in tgt_peers:
         push(fs_ref.at[p], fr_ref.at[t], f_send, f_recv, (s, p))
     fr_ref[t] = fs_ref[t]

time: 102 us -> 96.6 us (0.947)
  Pallas kernels: 101 us -> 95.1 us
    pallas_call x1, Pallas kernels: 101 us -> 95.1 us  [shards(): pl.pallas_call(sinkhorn_kernel, out_shape=jax.ShapeDtypeStruct((8, BLK),...]
where the time goes in v3:
time: 96.6 us; the launch traced here: 96.5 us
  Pallas kernels  95.1 us (98%)
  local copies, waits for them, and re-layouts  1.36 us (1%)
    pallas_call x1, Pallas kernels, shards(): pl.pallas_call(sinkhorn_kernel, out_shape=jax.ShapeDtypeStruct((8, BLK),...  95.1 us

profile of v3, /device:TPU:1, one launch (start us, length us, event | category | flops | bytes accessed | tf_op | source)
XLA Modules:
  0.0 96.5 jit_solution(3338290221648291520)
XLA Ops:
  0.0 95.1 %shard_map.100 = f32[8,128]{1,0:T(8,128)} custom-call(bf16[64,256]{1,0:T(8,128)(2,1)} %x_hbm.1, s32[8,64]{1,0:T(8,128)} %bitcast.12, s32[1,64]{1,0:T(1,128)} %bitcast.14, bf16[1024,256]{1,0:T(8,128)(2,1)} %t_hbm.1, s32[8,1024]{1,0:T(8,128)} %bitcast.10, s32[1,1024]{1,0:T(1,128)} %bitcast.13, bf16[256,256]{1,0:T(8,128)(2,1)} %ws_hbm.1, ...), custom_call_target="tpu_custom_call" | custom-call | tf_op jit(solution)/shard_map/pallas_call | solution.py:500
  95.1 0.8 reshape.14
  95.9 0.6 copy.13

commit v4 on v3

--- a/solution.py
+++ b/solution.py
@@ -285,7 +285,7 @@
             ht_ref[2 * pair + 1] = coded[:, BLK:]
             return 0
 
-        lax.fori_loop(0, 8, add_pair, 0)
+        lax.fori_loop(0, 8, add_pair, 0, unroll=4)
 
     to_scalar.wait()
     block_id = lax.broadcasted_iota(jnp.int32, (R_BLK, BLK), 0)
@@ -390,7 +390,7 @@
         return jnp.where(lane == c, high, tops), jnp.where(lane == c, total, sums)
 
     zero_tile = jnp.zeros((BLK, BLK), F32)
-    tops, sums = lax.fori_loop(0, C_LOC, first_cols, (zero_tile, zero_tile), unroll=2)
+    tops, sums = lax.fori_loop(0, C_LOC, first_cols, (zero_tile, zero_tile), unroll=4)
     tops = tops.T[:C_LOC]
     sums = sums.T[:C_LOC]
     cx_ref[0, s] = jnp.where(sums > 0.0, tops + jnp.log(sums), NEG)
@@ -416,7 +416,7 @@
                 total = total + jnp.where(block_id == row_of(c, m), part, 0.0)
             return total
 
-        total = lax.fori_loop(0, C_LOC, rows_of, jnp.zeros((R_BLK, BLK), F32), unroll=4)
+        total = lax.fori_loop(0, C_LOC, rows_of, jnp.zeros((R_BLK, BLK), F32), unroll=8)
         slot = 1 if rows_buf is rx_ref else sweep - 1
         rows_buf[slot, t] = total.astype(rows_buf.dtype)
         send_rows(sweep, rows_buf, slot)
@@ -431,7 +431,7 @@
                 total = total + e_ref[c * MOST + m] * u_ref[pl.ds(r, 1), :]
             return jnp.where(lane == c, jnp.sum(total, axis=1, keepdims=True), sums)
 
-        sums = lax.fori_loop(0, C_LOC, cols_of, zero_tile, unroll=4).T[:C_LOC]
+        sums = lax.fori_loop(0, C_LOC, cols_of, zero_tile, unroll=8).T[:C_LOC]
         cx_ref[sweep, s] = sums * factor
         send_cols(sweep)
         return row_scale, share / jnp.sum(await_cols(sweep), axis=0)

time: 96.6 us -> 90.3 us (0.935)
  Pallas kernels: 95.1 us -> 88.8 us
    pallas_call x1, Pallas kernels: 95.1 us -> 88.8 us  [shards(): pl.pallas_call(sinkhorn_kernel, out_shape=jax.ShapeDtypeStruct((8, BLK),...]
where the time goes in v4:
time: 90.3 us; the launch traced here: 90.2 us
  Pallas kernels  88.8 us (98%)
  local copies, waits for them, and re-layouts  1.36 us (2%)
    pallas_call x1, Pallas kernels, shards(): pl.pallas_call(sinkhorn_kernel, out_shape=jax.ShapeDtypeStruct((8, BLK),...  88.8 us

profile of v4, /device:TPU:1, one launch (start us, length us, event | category | flops | bytes accessed | tf_op | source)
XLA Modules:
  0.0 90.2 jit_solution(13409516841106530818)
XLA Ops:
  0.0 88.8 %shard_map.100 = f32[8,128]{1,0:T(8,128)} custom-call(bf16[64,256]{1,0:T(8,128)(2,1)} %x_hbm.1, s32[8,64]{1,0:T(8,128)} %bitcast.12, s32[1,64]{1,0:T(1,128)} %bitcast.14, bf16[1024,256]{1,0:T(8,128)(2,1)} %t_hbm.1, s32[8,1024]{1,0:T(8,128)} %bitcast.10, s32[1,1024]{1,0:T(1,128)} %bitcast.13, bf16[256,256]{1,0:T(8,128)(2,1)} %ws_hbm.1, ...), custom_call_target="tpu_custom_call" | custom-call | tf_op jit(solution)/shard_map/pallas_call | solution.py:500
  88.8 0.8 reshape.14
  89.6 0.6 copy.13

commit v5 on v4

--- a/solution.py
+++ b/solution.py
@@ -285,7 +285,7 @@
             ht_ref[2 * pair + 1] = coded[:, BLK:]
             return 0
 
-        lax.fori_loop(0, 8, add_pair, 0, unroll=4)
+        lax.fori_loop(0, 8, add_pair, 0, unroll=8 if step == NY - 1 else 4)
 
     to_scalar.wait()
     block_id = lax.broadcasted_iota(jnp.int32, (R_BLK, BLK), 0)
@@ -302,7 +302,7 @@
             best = jnp.maximum(best, jnp.where(block_id == r, jnp.max(raw, axis=0, keepdims=True), NEG))
         return best
 
-    top = lax.fori_loop(0, C_LOC, score_block, neg16, unroll=2)
+    top = lax.fori_loop(0, C_LOC, score_block, neg16, unroll=8)
     top_ref[...] = top
 
     def first_rows(c, total):
@@ -313,7 +313,7 @@
             total = total + jnp.where(block_id == r, part, 0.0)
         return total
 
-    total = lax.fori_loop(0, C_LOC, first_rows, jnp.zeros((R_BLK, BLK), F32), unroll=4)
+    total = lax.fori_loop(0, C_LOC, first_rows, jnp.zeros((R_BLK, BLK), F32), unroll=8)
     rx_ref[0, t] = jnp.where(total > 0.0, top + jnp.log(total), NEG)
 
     def send_rows(sweep, buf, slot):
@@ -357,7 +357,7 @@
             g_ref[slot, rows, :] = jnp.where(sid_ref[r, rows, :] == slot, value, 0.0)
         return 0
 
-    lax.fori_loop(0, SLOTS, pick, 0, unroll=2)
+    lax.fori_loop(0, SLOTS, pick, 0, unroll=4)
 
     def merge(block, _):
         total = jnp.zeros((QRY, BLK), F32)
@@ -463,13 +463,10 @@
         fs_ref[2 * block + 1] = jnp.where(lane8 < ROWS, pltpu.roll(low, ROWS, 1), high)
         return 0
 
-    lax.fori_loop(0, R_BLK, finish, 0, unroll=4)
+    lax.fori_loop(0, R_BLK, finish, 0, unroll=8)
     for p in tgt_peers:
         push(fs_ref.at[p], fr_ref.at[t], f_send, f_recv, (s, p))
     fr_ref[t] = fs_ref[t]
-    drain(fr_ref.at[pl.ds(0, NTGT - 1)], f_recv)
-    out_ref[...] = jnp.sum(fr_ref[...], axis=0)
-
     drain(big_x.at[pl.ds(0, 7 * A_ROWS)], a_send)
     drain(big_x.at[pl.ds(0, 3 * B_ROWS)], b_send)
     drain(big_x.at[pl.ds(0, 24 * A_ROWS)], ya_send)
@@ -479,6 +476,9 @@
         rows_sent = rh_ref.at[sweep - 1] if 0 < sweep < SWEEPS - 1 else rx_ref.at[min(sweep, 1)]
         drain(rows_sent.at[pl.ds(0, NTGT - 1)], r_send.at[sweep])
         drain(cx_ref.at[sweep, pl.ds(0, NSRC - 1)], c_send.at[sweep])
+    drain(fr_ref.at[pl.ds(0, NTGT - 1)], f_recv)
+    out_ref[...] = jnp.sum(fr_ref[...], axis=0)
+
     drain(fs_ref.at[pl.ds(0, NTGT - 1)], f_send)
 
 

time: 90.3 us -> 89.1 us (0.987)
  Pallas kernels: 88.8 us -> 87.6 us
    pallas_call x1, Pallas kernels: 88.8 us -> 87.6 us  [shards(): pl.pallas_call(sinkhorn_kernel, out_shape=jax.ShapeDtypeStruct((8, BLK),...]
where the time goes in v5:
time: 89.1 us; the launch traced here: 89 us
  Pallas kernels  87.6 us (98%)
  local copies, waits for them, and re-layouts  1.36 us (2%)
    pallas_call x1, Pallas kernels, shards(): pl.pallas_call(sinkhorn_kernel, out_shape=jax.ShapeDtypeStruct((8, BLK),...  87.6 us

profile of v5, /device:TPU:1, one launch (start us, length us, event | category | flops | bytes accessed | tf_op | source)
XLA Modules:
  0.0 89.0 jit_solution(16124654636316370811)
XLA Ops:
  0.0 87.6 %shard_map.100 = f32[8,128]{1,0:T(8,128)} custom-call(bf16[64,256]{1,0:T(8,128)(2,1)} %x_hbm.1, s32[8,64]{1,0:T(8,128)} %bitcast.12, s32[1,64]{1,0:T(1,128)} %bitcast.14, bf16[1024,256]{1,0:T(8,128)(2,1)} %t_hbm.1, s32[8,1024]{1,0:T(8,128)} %bitcast.10, s32[1,1024]{1,0:T(1,128)} %bitcast.13, bf16[256,256]{1,0:T(8,128)(2,1)} %ws_hbm.1, ...), custom_call_target="tpu_custom_call" | custom-call | tf_op jit(solution)/shard_map/pallas_call | solution.py:500
  87.6 0.8 reshape.14
  88.4 0.6 copy.13
